TPU v7x, 512 devices: a whole 4x8x8 slice. The times are simulated.
512 devices in a mesh: seq: 2 (over z_hi), ri: 16 (over y, core), rj: 16 (over z_lo, x).
Axes of the slice: x: 4, y: 8, z: 8 (z_hi: 2, z_lo: 4; z = z_hi * 4 + z_lo), core: 2. Of those that a mesh axis runs over, the one named last changes fastest.
Arguments:
- homolog_embedding: bfloat16 [512, 1024, 256], P('seq', ('ri', 'rj')), may hold values from -6 to 6
- standardizer_scaling: float32 [256], replicated, may hold values from 0.1 to 1.9
- standardizer_shift: float32 [256], replicated, may hold values from -3 to 3
- paired_projector_matrix: bfloat16 [256, 64], replicated, may hold values from -0.375 to 0.375
- final_projector_matrix: bfloat16 [1024, 128], replicated, may hold values from -4 to 4
- final_offset_vector: float32 [128], replicated, may hold values from -3 to 3
Outputs:
- pair_update: bfloat16 [1024, 1024, 128], P(('ri', 'seq'), 'rj')
All inputs are finite; a program needn't handle non-finite values.
Results may differ from a plain program's by a relative error of at most 0.0049.
Values may be sent and summed in bfloat16 or wider, within the bound.
A program may use at most 64 MiB of HBM per device.

v0:
```python
import math

import jax
import jax.numpy as jnp
from jax import lax
from jax.sharding import PartitionSpec as P


def spread_2(value, axis, source):
    kept = jnp.where(lax.axis_index(axis) == source, value, 0).astype(value.dtype)
    return lax.psum(kept, axis)


def standardize_features(homolog_embedding, standardizer_scaling, standardizer_shift):
    element_number = homolog_embedding.astype(jnp.float32)
    centre = jnp.mean(element_number, axis=-1, keepdims=True)
    spread = jnp.mean((element_number - centre) ** 2, axis=-1, keepdims=True)
    return (
        (element_number - centre) * lax.rsqrt(spread + 1e-05) * standardizer_scaling
        + standardizer_shift
    ).astype(jnp.bfloat16)


def pair_terms(left_part, right_part, final_projector_matrix, seq_total):
    depth, row_count, width = left_part.shape
    col_count = right_part.shape[1]
    block_rows = math.gcd(8, row_count)
    block_count = row_count // block_rows
    left_blocks = left_part.reshape(depth, block_count, block_rows, width).transpose(1, 0, 2, 3)

    def one_block(left_rows):
        outer = (
            jnp.einsum("sic,sjd->ijcd", left_rows, right_part, preferred_element_type=jnp.float32)
            / seq_total
        )
        outer = outer.astype(jnp.bfloat16).reshape(block_rows * col_count, width * width)
        return jnp.dot(outer, final_projector_matrix, preferred_element_type=jnp.float32)

    terms = lax.map(one_block, left_blocks)
    return terms.reshape(row_count, col_count, final_projector_matrix.shape[1])


def per_device(
    homolog_embedding,
    standardizer_scaling,
    standardizer_shift,
    paired_projector_matrix,
    final_projector_matrix,
    final_offset_vector,
):
    shard_homologs, shard_positions, feature_depth = homolog_embedding.shape
    width = paired_projector_matrix.shape[1] // 2
    standardized_embedding = standardize_features(
        homolog_embedding, standardizer_scaling, standardizer_shift
    )
    projected = jnp.dot(
        standardized_embedding.reshape(shard_homologs * shard_positions, feature_depth),
        paired_projector_matrix,
        preferred_element_type=jnp.float32,
    )
    projected = projected.astype(jnp.bfloat16).reshape(shard_homologs, shard_positions, 2 * width)
    row_block = lax.all_gather(projected, "rj", axis=1, tiled=True)
    left_rows = row_block[..., :width]
    right_here = row_block[..., width:]
    right_cols = spread_2(right_here, "ri", lax.axis_index("rj"))
    seq_groups = lax.axis_size("seq")
    seq_total = seq_groups * shard_homologs
    terms = pair_terms(left_rows, right_cols, final_projector_matrix, seq_total)
    summed = lax.psum_scatter(terms, "seq", scatter_dimension=0, tiled=True)
    return (summed + final_offset_vector).astype(jnp.bfloat16)


def solution(mesh):
    in_specs = (P("seq", ("ri", "rj"), None), P(), P(), P(), P(), P())
    out_specs = P(("ri", "seq"), "rj", None)
    return jax.shard_map(
        per_device, mesh=mesh, in_specs=in_specs, out_specs=out_specs, check_vma=False
    )
```

profile of v0, /device:TPU:1, one launch (start us, length us, event | category | flops | bytes accessed | tf_op | source)
XLA Modules:
  0.0 348.9 jit_solution(13037403438172516932)
XLA Ops:
  6.5 1.5 convert_reduce_fusion
  8.0 1.8 fusion.8
  9.8 1.4 fusion.11
  12.8 82.3 %all-gather.2.cloned.1.call-done = bf16[256,64,64]{0,2,1:T(8,128)(2,1)} async-done(((bf16[256,4,64]{0,2,1:T(8,128)(2,1)}), bf16[256,64,64]{0,2,1:T(8,128)(2,1)}) %all-gather.2.cloned.1.call-update) | async-done | bytes 2097168 | tf_op jit(solution)/shard_map/all_gather | solution.py:62
  95.1 3.0 slice_select_fusion
  98.2 124.4 %all-reduce.2.cloned.1.call-done = bf16[256,64,32]{0,2,1:T(8,128)(2,1)} async-done(((bf16[256,64,32]{0,2,1:T(8,128)(2,1)}), bf16[256,64,32]{0,2,1:T(8,128)(2,1)}) %all-reduce.2.cloned.1.call-update) | async-done | bytes 1048592 | tf_op jit(solution)/shard_map/psum | solution.py:11
  222.6 2.8 copy.16
  225.4 46.8 %while.10 = (s32[]{:T(128)}, f32[8,512,128]{2,1,0:T(8,128)}, bf16[8,256,8,32]{1,3,2,0:T(8,128)(2,1)}, bf16[256,64,32]{0,1,2:T(8,128)(2,1)}, bf16[1024,128]{1,0:T(8,128)(2,1)S(1)}, /*index=5*/s32[]{:T(128)}) while((s32[]{:T(128)}, f32[8,512,128]{2,1,0:T(8,128)}, bf16[8,256,8,32]{1,3,2,0:T(8,128)(2,1)}, bf16[256,64,32]{0,1,2:T(8,128)(2,1)}, ...), condition=%wide.region_4.5_spmd, body=%wide.region_3.4_spmd.sunk | while | flops 403701760 | bytes 7996485 | solution.py:39
  225.4 2.0 fusion.26
  227.4 1.4 copy.19
  231.2 2.0 fusion.26
  233.3 1.4 copy.19
  237.1 2.0 fusion.26
  239.1 1.4 copy.19
  242.9 2.0 fusion.26
  245.0 1.4 copy.19
  248.8 2.0 fusion.26
  250.8 1.4 copy.19
  254.6 2.0 fusion.26
  260.5 2.0 fusion.26
  266.3 2.0 fusion.26
  268.3 1.4 copy.19
  272.2 68.0 %reduce-scatter.2.cloned.1.call-done = f32[32,64,128]{2,1,0:T(8,128)} async-done(((f32[64,64,128]{2,1,0:T(8,128)}), f32[32,64,128]{2,1,0:T(8,128)}) %reduce-scatter.2.cloned.1.call-update) | async-done | bytes 1048592 | tf_op jit(solution)/shard_map/reduce_scatter | solution.py:69
  340.2 2.2 add_convert_fusion
  (39 shorter events, 23.8 us)
Async XLA Ops:
  6.5 4.9 %copy-start = (bf16[256,64]{0,1:T(8,128)(2,1)S(1)}, bf16[256,64]{0,1:T(8,128)(2,1)}, u32[]{:S(2)}) copy-start(bf16[256,64]{0,1:T(8,128)(2,1)} %param.11) | copy-start | bytes 98308
  6.5 3.3 copy-start.2
  6.5 88.5 %all-gather.2.cloned.1.call-start = ((), (), s32[]{:S(2)}) async-start(), calls=%async_computation.1 | async-start | bytes 2228224 | tf_op jit(solution)/shard_map/all_gather | solution.py:62
  12.7 209.9 %all-reduce.2.cloned.1.call-start = ((), (), s32[]{:S(2)}) async-start(), calls=%async_computation.2 | async-start | bytes 2097152 | tf_op jit(solution)/shard_map/psum | solution.py:11
  98.1 127.3 %copy-start.1 = (bf16[1024,128]{1,0:T(8,128)(2,1)S(1)}, bf16[1024,128]{1,0:T(8,128)(2,1)}, u32[]{:S(2)}) copy-start(bf16[1024,128]{1,0:T(8,128)(2,1)} %param.12) | copy-start | bytes 786436
  98.1 242.1 %reduce-scatter.2.cloned.1.call-start = ((), (), s32[]{:S(2)}) async-start(), calls=%async_computation.3 | async-start | bytes 3145728 | tf_op jit(solution)/shard_map/reduce_scatter | solution.py:69
  272.2 68.0 %copy-start.3 = (f32[128]{0:T(128)S(1)}, f32[128]{0:T(128)}, u32[]{:S(2)}) copy-start(f32[128]{0:T(128)} %param.13) | copy-start | bytes 1540
Sparse Core Ops, SparseCore 0:
  12.8 82.1 all-gather.1
  98.2 124.3 all-reduce.1
  272.3 67.8 reduce-scatter.1
where the time goes:
time: 349 us
  waiting for transfers between devices  275 us (79%)
  matrix products  25.9 us (7%)
  local copies, waits for them, and re-layouts  24.8 us (7%)
  between operations  13.2 us (4%)
  other arithmetic  9.84 us (3%)
    psum x1, waiting for transfers between devices, spread_2(): return lax.psum(kept, axis)  124 us
    all_gather x1, waiting for transfers between devices, per_device(): row_block = lax.all_gather(projected, 'rj', axis=1, tiled=True)  82.3 us
    reduce_scatter x1, waiting for transfers between devices, per_device(): summed = lax.psum_scatter(terms, 'seq', scatter_dimension=0, tiled=True)  68 us
    dot_general x8, matrix products, one_block(): jnp.einsum('sic,sjd->ijcd', left_rows, right_part, preferred_element_type...  16.2 us
    convert_element_type x8, local copies, waits for them, and re-layouts, one_block(): outer.astype(jnp.bfloat16).reshape(block_rows * col_count, width * width)  10.8 us
    reshape x8, local copies, waits for them, and re-layouts, one_block(): outer.astype(jnp.bfloat16).reshape(block_rows * col_count, width * width)  10.1 us
    dot_general x8, matrix products, one_block(): jnp.dot(outer, final_projector_matrix, preferred_element_type=jnp.float32)  9.45 us
  transfers between devices with their start and end apart: 3, of which 3 were waited for; matrix products, arithmetic and copies ran while one was open for 0% of the time, Pallas kernels for 0%

commit v1 on v0

v1 whole, which is shorter than its diff:
```python
import jax
import jax.numpy as jnp
from jax import lax
from jax.experimental import pallas as pl
from jax.experimental.pallas import tpu as pltpu
from jax.sharding import PartitionSpec as P

F32 = jnp.float32
BF16 = jnp.bfloat16
MESH = pl.DeviceIdType.MESH
NT = (((1,), (1,)), ((), ()))


def remote(src, dst, send_sem, recv_sem, dev):
    return pltpu.make_async_remote_copy(
        src_ref=src, dst_ref=dst, send_sem=send_sem, recv_sem=recv_sem, device_id=dev, device_id_type=MESH
    )


def standardize(x, gain, shift):
    centre = jnp.mean(x, axis=-1, keepdims=True)
    away = x - centre
    spread = jnp.mean(away * away, axis=-1, keepdims=True)
    return (away * lax.rsqrt(spread + 1e-05) * gain + shift).astype(BF16)


def project(x_ref, gain, shift, w64, lsend, rsend):
    pieces = []
    for k in range(4):
        normed = standardize(x_ref[k].astype(F32), gain[...], shift[...])
        both = lax.dot_general(w64[...], normed, NT, preferred_element_type=F32)
        lsend[k * 32:(k + 1) * 32, :] = both[:32].astype(BF16)
        pieces.append(both[32:])
    for dc in range(4):
        rows = jnp.concatenate([p[dc * 8:(dc + 1) * 8] for p in pieces], axis=0).astype(BF16)
        for sl in range(2):
            rsend[sl, dc] = rows[:, sl * 128:(sl + 1) * 128]


def arrange_final(wfin, wide, w2t):
    wide[...] = wfin[...].astype(F32)
    for d2 in range(2):
        rows = jnp.concatenate([wide[pl.ds(dp * 2 + d2, 32, stride=32), :] for dp in range(16)], axis=0)
        w2t[d2 * 128:(d2 + 1) * 128, :] = rows.T.astype(BF16)


def pair_rows(ib, lt, rt, w2t, outer, off, out, scale):
    rows = pl.ds(pl.multiple_of(ib * 256, 256), 256)
    left = jnp.concatenate([lt[0, rows, :], lt[1, rows, :]], axis=1)
    for dc in range(4):
        right = jnp.concatenate([rt[s, dc * 512:(dc + 1) * 512, :] for s in range(4)], axis=1)
        p = lax.dot_general(left, right, NT, preferred_element_type=F32).astype(BF16)
        for i in range(8):
            for dp in range(4):
                outer[(dc * 4 + dp) * 32:(dc * 4 + dp + 1) * 32, i * 128:(i + 1) * 128] = p[
                    i * 32:(i + 1) * 32, dp * 128:(dp + 1) * 128
                ]
    res = jnp.dot(w2t[...], outer[...], preferred_element_type=F32)
    first = lax.broadcasted_iota(jnp.int32, (128, 128), 1) < 64
    for i in range(8):
        both = jnp.where(first, res[:128, i * 128:(i + 1) * 128], res[128:, i * 128:(i + 1) * 128]).T
        out[ib * 8 + i] = ((both[:64] + both[64:]) * scale + off[...]).astype(BF16)


def kernel(x_ref, gain, shift, w64, wfin, off, out,
           lt, rt, lsend, rsend, stage, stage_f, wide, w2t, outer,
           z_send, z_recv, x_send, x_recv, s_send, s_recv, a_send, a_recv, b_send, b_recv, p_send, p_recv):
    q, ri, rj = lax.axis_index("seq"), lax.axis_index("ri"), lax.axis_index("rj")
    y, c, zl, xx = ri // 2, ri % 2, rj // 4, rj % 4
    half = zl // 2
    way = 1 - 2 * c
    self_z = half == q
    self_s = jnp.logical_and(rj == ri, (ri % 4) // 2 == q)

    def at_x(n):
        return (q, ri, zl * 4 + (xx + n + 4) % 4)

    def at_y(n):
        return (q, 2 * ((y + n + 8) % 8) + c, rj)

    peer = (q, 2 * y + 1 - c, rj)

    barrier = pltpu.get_barrier_semaphore()

    def greet(dev):
        pl.semaphore_signal(barrier, inc=1, device_id=dev, device_id_type=MESH)

    for a in range(2):
        for b in range(2):
            me = jnp.logical_and(a == q, 2 * q + b == zl)

            @pl.when(jnp.logical_not(me))
            def _():
                greet((a, ri, 4 * (2 * q + b) + xx))

    for n in (1, -1):
        greet(at_x(n))
        greet(at_y(n))
    greet(peer)

    def greet_source(s, carry):
        me = jnp.logical_and(self_s, s == rj)

        @pl.when(jnp.logical_not(me))
        def _():
            greet(((ri % 4) // 2, rj, s))

        return carry

    lax.fori_loop(0, 16, greet_source, 0)

    project(x_ref, gain, shift, w64, lsend, rsend)

    pl.semaphore_wait(barrier, 25 - self_z.astype(jnp.int32) - self_s.astype(jnp.int32))

    def scatter(n, dc, sl, qd):
        dev = (qd, 4 * dc + 2 * q + sl, ri)
        me = jnp.logical_and(jnp.logical_and(qd == q, rj == ri), 4 * dc + 2 * q + sl == ri)
        dst = stage.at[pl.ds(pl.multiple_of(rj * 32, 32), 32), :]
        return me, remote(rsend.at[sl, dc], dst, s_send.at[n], s_recv.at[rj], dev), pltpu.make_async_copy(
            rsend.at[sl, dc], dst, s_recv.at[rj]
        )

    combos = [(dc, sl, qd) for dc in range(4) for sl in range(2) for qd in range(2)]
    for n, combo in enumerate(combos):
        me, far, near = scatter(n, *combo)

        @pl.when(me)
        def _():
            near.start()

        @pl.when(jnp.logical_not(me))
        def _():
            far.start()

    z_slot = lt.at[q, pl.ds(pl.multiple_of(((zl % 2) * 4 + xx) * 128, 128), 128), :]
    z_sem = z_recv.at[q * 2 + zl % 2]

    def z_copy(t):
        return remote(lsend, z_slot, z_send.at[t], z_sem, (half, ri, 4 * ((zl + t) % 4) + xx))

    for t in (3, 2, 1):
        z_copy(t).start()

    @pl.when(self_z)
    def _():
        pltpu.make_async_copy(lsend, z_slot, z_sem).start()

    @pl.when(jnp.logical_not(self_z))
    def _():
        z_copy(0).start()

    arrange_final(wfin, wide, w2t)

    def slot(m):
        return rt.at[m % 4, pl.ds(pl.multiple_of((m // 4) * 512, 512), 512), :]

    for s in range(16):
        piece = stage.at[s * 32:(s + 1) * 32, :]
        pltpu.make_async_copy(piece, piece, s_recv.at[s]).wait()
    stage_f[...] = stage[...].astype(F32)
    for d in range(8):
        rt[ri % 4, pl.ds(pl.multiple_of((ri // 4) * 512 + d * 64, 64), 64), :] = stage_f[
            pl.ds(d, 64, stride=8), :
        ].astype(BF16)

    def ring_a(k):
        s = slot(2 * ((y - way * k + 8) % 8) + c)
        return remote(s, s, a_send.at[k], a_recv.at[k], at_y(way))

    def ring_b(k):
        s = slot(2 * ((y + way * k + 8) % 8) + c)
        return remote(s, s, b_send.at[k], b_recv.at[k], at_y(-way))

    def here(n, step):
        s = slot(2 * ((y + step + 8) % 8) + c)
        return remote(s, s, p_send.at[n], p_recv.at[n], peer)

    def land(sem, m):
        s = slot(m)
        pltpu.make_async_copy(s, s, sem).wait()

    ring_a(0).start()
    ring_b(0).start()
    here(0, 0).start()

    def x_slot(a, b, n):
        return lt.at[a, pl.ds(pl.multiple_of((b * 4 + (xx + n + 4) % 4) * 128, 128), 128), :]

    def x_copy(a, b, n, ahead):
        g = (a * 2 + b) * 3
        if n == 0:
            return remote(x_slot(a, b, 0), x_slot(a, b, 0), x_send.at[g + ahead], x_recv.at[g + ahead],
                          at_x(way if ahead == 0 else -way))
        return remote(x_slot(a, b, -way), x_slot(a, b, -way), x_send.at[g + 2], x_recv.at[g + 2], at_x(way))

    def x_land(a, b, kind):
        s = x_slot(a, b, (-way, way, 2)[kind])
        pltpu.make_async_copy(s, s, x_recv.at[(a * 2 + b) * 3 + kind]).wait()

    pieces = [(a, b) for a in range(2) for b in range(2)]

    for a, b in pieces:
        s = x_slot(a, b, 0)
        pltpu.make_async_copy(s, s, z_recv.at[a * 2 + b]).wait()
        x_copy(a, b, 0, 0).start()
        x_copy(a, b, 0, 1).start()

    def ring_step(k):
        land(a_recv.at[k - 1], 2 * ((y - way * k + 8) % 8) + c)
        if k < 4:
            ring_a(k).start()
        here(k, -way * k).start()
        if k < 4:
            land(b_recv.at[k - 1], 2 * ((y + way * k + 8) % 8) + c)
            if k < 3:
                ring_b(k).start()
            here(4 + k, way * k).start()

    ring_step(1)
    for a, b in pieces:
        x_land(a, b, 0)
        x_copy(a, b, 1, 0).start()
    ring_step(2)
    ring_step(3)
    for a, b in pieces:
        x_land(a, b, 1)
        x_land(a, b, 2)
    ring_step(4)
    land(p_recv.at[0], 2 * y + 1 - c)
    for k in range(1, 5):
        land(p_recv.at[k], 2 * ((y + way * k + 8) % 8) + 1 - c)
    for k in range(1, 4):
        land(p_recv.at[4 + k], 2 * ((y - way * k + 8) % 8) + 1 - c)

    scale = 1.0 / (2 * x_ref.shape[1])

    def block(ib, carry):
        pair_rows(ib, lt, rt, w2t, outer, off, out, scale)
        return carry

    lax.fori_loop(0, 4, block, 0)

    for n, combo in enumerate(combos):
        me, far, near = scatter(n, *combo)

        @pl.when(jnp.logical_not(me))
        def _():
            far.wait_send()

    for t in (1, 2, 3):
        z_copy(t).wait_send()

    @pl.when(jnp.logical_not(self_z))
    def _():
        z_copy(0).wait_send()

    for k in range(4):
        ring_a(k).wait_send()
    for k in range(3):
        ring_b(k).wait_send()
    here(0, 0).wait_send()
    for k in range(1, 5):
        here(k, -way * k).wait_send()
    for k in range(1, 4):
        here(4 + k, way * k).wait_send()
    for a, b in pieces:
        x_copy(a, b, 0, 0).wait_send()
        x_copy(a, b, 0, 1).wait_send()
        x_copy(a, b, 1, 0).wait_send()


def per_device(embedding, gain, shift, projector, final, offset):
    dma = pltpu.SemaphoreType.DMA
    vmem = pl.BlockSpec(memory_space=pltpu.VMEM)
    return pl.pallas_call(
        kernel,
        out_shape=jax.ShapeDtypeStruct((32, 64, 128), BF16),
        in_specs=[vmem] * 6,
        out_specs=vmem,
        scratch_shapes=[
            pltpu.VMEM((2, 1024, 256), BF16),
            pltpu.VMEM((4, 2048, 128), BF16),
            pltpu.VMEM((128, 256), BF16),
            pltpu.VMEM((2, 4, 32, 128), BF16),
            pltpu.VMEM((512, 128), BF16),
            pltpu.VMEM((512, 128), F32),
            pltpu.VMEM((1024, 128), F32),
            pltpu.VMEM((256, 512), BF16),
            pltpu.VMEM((512, 1024), BF16),
            dma((4,)), dma((4,)), dma((12,)), dma((12,)), dma((16,)), dma((16,)),
            dma((4,)), dma((4,)), dma((3,)), dma((3,)), dma((8,)), dma((8,)),
        ],
        compiler_params=pltpu.CompilerParams(
            collective_id=0, has_side_effects=True, vmem_limit_bytes=48 << 20
        ),
    )(jnp.swapaxes(embedding, 0, 1), gain.reshape(1, -1), shift.reshape(1, -1), projector.T, final, offset.reshape(1, -1))


def solution(mesh):
    in_specs = (P("seq", ("ri", "rj"), None), P(), P(), P(), P(), P())
    return jax.shard_map(
        per_device, mesh=mesh, in_specs=in_specs, out_specs=P(("ri", "seq"), "rj", None), check_vma=False
    )
```

time: 349 us -> 54.9 us (0.16)
  waiting for transfers between devices: 275 us -> 0 us
  Pallas kernels: 0 us -> 52.1 us
  matrix products: 25.9 us -> 0 us
  local copies, waits for them, and re-layouts: 24.8 us -> 2.6 us
  between operations: 13.2 us -> 0.06 us
  other arithmetic: 9.84 us -> 0 us
    psum x1 -> x0, waiting for transfers between devices: 124 us -> none  [spread_2(): return lax.psum(kept, axis)]
    all_gather x1 -> x0, waiting for transfers between devices: 82.3 us -> none  [per_device(): row_block = lax.all_gather(projected, 'rj', axis=1, tiled=True)]
    reduce_scatter x1 -> x0, waiting for transfers between devices: 68 us -> none  [per_device(): summed = lax.psum_scatter(terms, 'seq', scatter_dimension=0, tiled=True)]
    pallas_call x0 -> x1, Pallas kernels: none -> 52.1 us  [per_device(): pl.pallas_call(kernel, out_shape=jax.ShapeDtypeStruct((32, 64, 128), BF16...]
    dot_general x17 -> x0, matrix products: 25.9 us -> none  [the longest x8 16.2 us: one_block(): jnp.einsum('sic,sjd->ijcd', left_rows, right_part, preferred_element_type...]
    reshape x10 -> x0, local copies, waits for them, and re-layouts: 11 us -> none  [the longest x8 10.1 us: one_block(): outer.astype(jnp.bfloat16).reshape(block_rows * col_count, width * width)]
    convert_element_type x9 -> x0, local copies, waits for them, and re-layouts: 11 us -> none  [the longest x8 10.8 us: one_block(): outer.astype(jnp.bfloat16).reshape(block_rows * col_count, width * width)]
    convert_element_type x2 -> x0, other arithmetic: 3.58 us -> none  [the longest x1 2.16 us: per_device(): return (summed + final_offset_vector).astype(jnp.bfloat16)]
  transfers between devices with their start and end apart: 3 -> 0, of which waited for: 3 -> 0; matrix products, arithmetic and copies ran while one was open for 0% -> 0% of each run, Pallas kernels for 0% -> 0%
where the time goes in v1:
time: 54.9 us; the launch traced here: 54.7 us
  Pallas kernels  52.1 us (95%)
  local copies, waits for them, and re-layouts  2.6 us (5%)
    pallas_call x1, Pallas kernels, per_device(): pl.pallas_call(kernel, out_shape=jax.ShapeDtypeStruct((32, 64, 128), BF16...  52.1 us
    unnamed x12, local copies, waits for them, and re-layouts  2.6 us

profile of v1, /device:TPU:1, one launch (start us, length us, event | category | flops | bytes accessed | tf_op | source)
XLA Modules:
  0.0 54.7 jit_solution(14070861845781157847)
XLA Ops:
  0.0 0.0 copy-start
  0.0 0.0 copy-start.1
  0.0 0.0 copy-start.3
  0.0 1.2 %copy.9 = bf16[256,4,256]{2,0,1:T(8,128)(2,1)S(1)} copy(bf16[256,4,256]{2,1,0:T(4,128)(2,1)} %param.6) | data formatting | bytes 1048576 | tf_op args[0]
  1.2 0.0 copy-start.2
  1.2 0.0 copy-start.4
  1.2 0.0 copy-done
  1.2 0.0 copy-done.1
  1.2 0.0 copy-done.3
  1.2 0.6 %copy-done.2 = f32[256]{0:T(256)S(1)} copy-done((f32[256]{0:T(256)S(1)}, f32[256]{0:T(256)}, u32[]{:S(2)}) %copy-start.2) | copy-done | bytes 1048
  1.9 0.0 copy-done.4
  1.9 52.1 %shard_map.64 = bf16[32,64,128]{2,1,0:T(8,128)(2,1)S(1)} custom-call(bf16[4,256,256]{2,1,0:T(8,128)(2,1)S(1)} %bitcast.7, f32[1,256]{1,0:T(1,128)S(1)} %bitcast.9, f32[1,256]{1,0:T(1,128)S(1)} %bitcast.10, bf16[64,256]{1,0:T(8,128)(2,1)S(1)} %bitcast.8, bf16[1024,128]{1,0:T(8,128)(2,1)S(1)} %copy-done, f32[1,128]{1,0:T(1,128)S(1)} %bitcast.11), custom_call_target="tpu_custom_call" | custom-call | tf_op jit(solution)/shard_map/pallas_call | solution.py:276
  53.9 0.8 %copy.11 = bf16[32,64,128]{2,1,0:T(8,128)(2,1)} copy(bf16[32,64,128]{2,1,0:T(8,128)(2,1)S(1)} %shard_map.64) | data formatting | bytes 1048576
Async XLA Ops:
  0.0 1.2 %copy-start = (bf16[1024,128]{1,0:T(8,128)(2,1)S(1)}, bf16[1024,128]{1,0:T(8,128)(2,1)}, u32[]{:S(2)}) copy-start(bf16[1024,128]{1,0:T(8,128)(2,1)} %wfin.1) | copy-start | bytes 786436
  0.0 1.2 %copy-start.1 = (bf16[256,64]{0,1:T(8,128)(2,1)S(1)}, bf16[256,64]{0,1:T(8,128)(2,1)}, u32[]{:S(2)}) copy-start(bf16[256,64]{0,1:T(8,128)(2,1)} %param.9) | copy-start | bytes 98308
  0.0 1.2 %copy-start.3 = (f32[256]{0:T(256)S(1)}, f32[256]{0:T(256)}, u32[]{:S(2)}) copy-start(f32[256]{0:T(256)} %param.8) | copy-start | bytes 3076
  1.2 0.7 %copy-start.2 = (f32[256]{0:T(256)S(1)}, f32[256]{0:T(256)}, u32[]{:S(2)}) copy-start(f32[256]{0:T(256)} %param.7) | copy-start | bytes 3076
  1.2 0.7 %copy-start.4 = (f32[128]{0:T(128)S(1)}, f32[128]{0:T(128)}, u32[]{:S(2)}) copy-start(f32[128]{0:T(128)} %param.11) | copy-start | bytes 1540

commit v2 on v1

v2 whole, which is shorter than its diff:
```python
import jax
import jax.numpy as jnp
from jax import lax
from jax.experimental import pallas as pl
from jax.experimental.pallas import tpu as pltpu
from jax.sharding import PartitionSpec as P

F32 = jnp.float32
BF16 = jnp.bfloat16
MESH = pl.DeviceIdType.MESH
NT = (((1,), (1,)), ((), ()))


def remote(src, dst, send_sem, recv_sem, dev):
    return pltpu.make_async_remote_copy(
        src_ref=src, dst_ref=dst, send_sem=send_sem, recv_sem=recv_sem, device_id=dev, device_id_type=MESH
    )


def standardize(x, gain, shift):
    centre = jnp.mean(x, axis=-1, keepdims=True)
    away = x - centre
    spread = jnp.mean(away * away, axis=-1, keepdims=True)
    return (away * lax.rsqrt(spread + 1e-05) * gain + shift).astype(BF16)


def project(x_ref, gain, shift, w64, lsend, rsend):
    pieces = []
    for k in range(4):
        normed = standardize(x_ref[k].astype(F32), gain[...], shift[...])
        both = lax.dot_general(w64[...], normed, NT, preferred_element_type=F32)
        lsend[k * 32:(k + 1) * 32, :] = both[:32].astype(BF16)
        pieces.append(both[32:])
    for dc in range(4):
        rows = jnp.concatenate([p[dc * 8:(dc + 1) * 8] for p in pieces], axis=0).astype(BF16)
        for sl in range(2):
            rsend[sl, dc] = rows[:, sl * 128:(sl + 1) * 128]


def arrange_final(wfin, wide, w2t):
    wide[...] = wfin[...].astype(F32)
    for d2 in range(2):
        rows = jnp.concatenate([wide[pl.ds(dp * 2 + d2, 32, stride=32), :] for dp in range(16)], axis=0)
        turned = rows.T.astype(BF16)
        for dc in range(4):
            w2t[dc, d2 * 128:(d2 + 1) * 128, :] = turned[:, dc * 128:(dc + 1) * 128]


def outer_product(ib, pos, dc, lt, rt, outer):
    rows = pl.ds(pl.multiple_of(ib * 256, 256), 256)
    left = jnp.concatenate([lt[0, rows, :], lt[1, rows, :]], axis=1)
    right = jnp.concatenate([rt[sc, pl.ds(dc * 8, 8)].reshape(512, 128) for sc in range(4)], axis=1)
    p = lax.dot_general(left, right, NT, preferred_element_type=F32).astype(BF16)
    for i in range(8):
        for dp in range(4):
            outer[ib, (pos * 4 + dp) * 32:(pos * 4 + dp + 1) * 32, i * 128:(i + 1) * 128] = p[
                i * 32:(i + 1) * 32, dp * 128:(dp + 1) * 128
            ]


def last_product(ib, t, dcs, w2t, outer):
    weights = jnp.concatenate([w2t[dc] for dc in dcs], axis=1)
    res = jnp.dot(weights, outer[ib, t * 256:(t + 1) * 256, :], preferred_element_type=F32)
    lane = lax.broadcasted_iota(jnp.int32, (128, 1024), 1)
    return jnp.where(lane % 128 < 64, res[:128], res[128:])


def kernel(x_ref, gain, shift, w64, wfin, off, out,
           lt, rt, lsend, rsend, stage, stage_f, wide, w2t, outer, partial,
           z_send, z_recv, f_send, x_send, x_recv, s_send, s_recv, a_send, a_recv, b_send, b_recv, p_send, p_recv):
    q, ri, rj = lax.axis_index("seq"), lax.axis_index("ri"), lax.axis_index("rj")
    y, c, zl, xx = ri // 2, ri % 2, rj // 4, rj % 4
    half = zl // 2
    way = 1 - 2 * c
    self_z = half == q
    self_s = rj == ri

    def at_x(n):
        return (q, ri, zl * 4 + (xx + n + 4) % 4)

    def at_y(n):
        return (q, 2 * ((y + n + 8) % 8) + c, rj)

    def at_w(h, w):
        return (h, ri, (w + h * (3 - 2 * w)) * 4 + xx)

    peer = (q, 2 * y + 1 - c, rj)
    place = zl + q * (3 - 2 * zl)
    src = 4 * (q + half - 2 * q * half) + (zl % 2 + half - 2 * (zl % 2) * half)

    barrier = pltpu.get_barrier_semaphore()

    def greet(dev):
        pl.semaphore_signal(barrier, inc=1, device_id=dev, device_id_type=MESH)

    def greet_source(s, carry):
        for a in range(2):
            me = jnp.logical_and(self_s, jnp.logical_and(a == q, s == rj))

            @pl.when(jnp.logical_not(me))
            def _():
                greet((a, rj, s))

        return carry

    lax.fori_loop(0, 16, greet_source, 0)

    def greet_place(w):
        @pl.when(w >= 0)
        def _():
            greet((jnp.where(w >= 4, 1 - q, q), ri, jnp.where(q == 0, w % 4, 3 - w % 4) * 4 + xx))

    def table(*values):
        v = values[3]
        for n in (2, 1, 0):
            v = jnp.where(place == n, values[n], v)
        return v

    greet_place(table(1, 0, 0, 1))
    greet_place(table(5, 4, 1, 4))
    greet_place(table(1, 0, 5, 2))
    greet_place(table(-1, -1, 3, 2))
    for n in (1, -1):
        greet(at_x(n))
        greet(at_y(n))
    greet(peer)

    project(x_ref, gain, shift, w64, lsend, rsend)

    z_targets = jnp.where(src == 1, 3, 2) + jnp.where(place == 2, 2, 1)
    pl.semaphore_wait(barrier, 32 - self_s.astype(jnp.int32) + z_targets + 5)

    def scatter(n, dc, sl, qd, yh):
        dev = (qd, 2 * (dc + 4 * yh) + sl, ri)
        me = jnp.logical_and(jnp.logical_and(qd == q, rj == ri), 2 * (dc + 4 * yh) + sl == ri)
        dst = stage.at[q, pl.ds(pl.multiple_of(rj * 32, 32), 32), :]
        sem = s_recv.at[q * 16 + rj]
        return me, remote(rsend.at[sl, dc], dst, s_send.at[n], sem, dev), pltpu.make_async_copy(
            rsend.at[sl, dc], dst, sem
        )

    combos = [(dc, sl, qd, yh) for dc in range(4) for sl in range(2) for qd in range(2) for yh in range(2)]
    for n, combo in enumerate(combos):
        me, far, near = scatter(n, *combo)

        @pl.when(me)
        def _():
            near.start()

        @pl.when(jnp.logical_not(me))
        def _():
            far.start()

    def left_slot(h, e, x):
        a = e // 2 + h - 2 * (e // 2) * h
        b = e % 2 + h - 2 * (e % 2) * h
        return lt.at[a, pl.ds(pl.multiple_of((b * 4 + x) * 128, 128), 128), :]

    own = src % 4 + 2 * (src // 4)
    z_slot = left_slot(half, own, xx)

    def z_copy(t):
        w = (1 - src % 2, jnp.where(src == 4, 3, 2), 3)[t]
        return remote(lsend, z_slot, z_send.at[t], z_recv.at[own], at_w(half, w))

    z_copy(1).start()

    @pl.when(src == 1)
    def _():
        z_copy(2).start()

    z_copy(0).start()

    @pl.when(self_z)
    def _():
        pltpu.make_async_copy(lsend, z_slot, z_recv.at[own]).start()

    arrange_final(wfin, wide, w2t)

    order = [table(0, 1, 1, 2), table(1, 0, 0, 1), table(3, 2, 3, 0), table(2, 3, 2, 3)]
    passing = [place == 3, place == 2, place <= 2]

    def onward(p):
        e = order[p]
        s = left_slot(q, e, xx)
        return remote(s, s, f_send.at[p], z_recv.at[e], at_w(q, place + 1 - 2 * (place % 2)))

    def x_copy(p, kind):
        e = order[p]
        s = left_slot(q, e, xx if kind < 2 else (xx - way + 4) % 4)
        return remote(s, s, x_send.at[e * 3 + kind], x_recv.at[e * 3 + kind], at_x(-way if kind == 1 else way))

    def x_land(p, kind):
        e = order[p]
        s = left_slot(q, e, (xx + (-way, way, 2)[kind] + 4) % 4)
        pltpu.make_async_copy(s, s, x_recv.at[e * 3 + kind]).wait()

    def z_land(p):
        e = order[p]
        s = left_slot(q, e, xx)
        pltpu.make_async_copy(s, s, z_recv.at[e]).wait()
        if p < 3:
            @pl.when(passing[p])
            def _():
                onward(p).start()
        x_copy(p, 0).start()
        x_copy(p, 1).start()

    def x_step(p):
        x_land(p, 0)
        x_copy(p, 2).start()

    near_zl = (zl, zl + 1 - 2 * (zl % 2), (zl + 2) % 4, 3 - zl)
    parts = [(q, near_zl[n]) for n in (0, 1, 2, 3)] + [(1 - q, near_zl[n]) for n in (3, 2, 1, 0)]

    def part(step, g):
        a, z = parts[g]
        return rt.at[2 * a + c, pl.ds(((y + step + 8) % 4) * 8, 8), pl.ds(pl.multiple_of(z * 16, 16), 16), :]

    def quarter(step, a, core):
        return rt.at[2 * a + core, pl.ds(((y + step + 8) % 4) * 8, 8)]

    def ring_a(k, g):
        s = part(-way * k, g)
        return remote(s, s, a_send.at[k * 8 + g], a_recv.at[k * 8 + g], at_y(way))

    def ring_b(g):
        s = part(0, g)
        return remote(s, s, b_send.at[g], b_recv.at[g], at_y(-way))

    steps = (0, -1, 1, -2)

    def here(kind, n):
        a = parts[n * 4][0]
        s = quarter(way * steps[kind], a, c)
        return remote(s, s, p_send.at[kind * 2 + a], p_recv.at[kind * 2 + a], peer)

    def here_land(kind):
        for a in range(2):
            s = quarter(-way * steps[kind], a, 1 - c)
            pltpu.make_async_copy(s, s, p_recv.at[kind * 2 + a]).wait()

    def land(sem, s):
        pltpu.make_async_copy(s, s, sem).wait()

    def assemble(g):
        a, z = parts[g]
        for x in range(4):
            piece = stage.at[a, pl.ds(pl.multiple_of((z * 4 + x) * 32, 32), 32), :]
            land(s_recv.at[a * 16 + z * 4 + x], piece)
        stage_f[g] = stage[a, pl.ds(pl.multiple_of(z * 128, 128), 128), :].astype(F32)
        for d in range(8):
            rt[2 * a + c, (y % 4) * 8 + d, pl.ds(pl.multiple_of(z * 16, 16), 16), :] = stage_f[
                g, pl.ds(d, 16, stride=8), :
            ].astype(BF16)
        ring_a(0, g).start()
        ring_b(g).start()
        if g % 4 == 3:
            here(0, g // 4).start()

    def pass_on(g):
        land(a_recv.at[g], part(-way, g))
        ring_a(1, g).start()
        land(b_recv.at[g], part(way, g))
        if g % 4 == 3:
            here(1, g // 4).start()
            here(2, g // 4).start()

    z_land(0)
    z_land(1)
    for g in range(4):
        assemble(g)
    z_land(2)
    for g in range(4, 8):
        assemble(g)
    z_land(3)
    for g in range(8):
        pass_on(g)
        if g % 2 == 1:
            x_step(g // 2)
    for p in range(4):
        x_land(p, 1)
        x_land(p, 2)
    for kind in range(3):
        here_land(kind)

    dcs = [(y + n) % 4 for n in (0, 1, 3, 2)]

    def early(ib, carry):
        for pos in range(3):
            outer_product(ib, pos, dcs[pos], lt, rt, outer)
        partial[ib] = last_product(ib, 0, dcs[:2], w2t, outer)
        return carry

    lax.fori_loop(0, 4, early, 0)

    for g in range(8):
        land(a_recv.at[8 + g], part(-way * 2, g))
        if g % 4 == 3:
            here(3, g // 4).start()
    here_land(3)

    scale = 1.0 / (2 * x_ref.shape[1])

    def late(ib, carry):
        outer_product(ib, 3, dcs[3], lt, rt, outer)
        total = partial[ib] + last_product(ib, 1, dcs[2:], w2t, outer)
        for i in range(8):
            both = total[:, i * 128:(i + 1) * 128].T
            out[ib * 8 + i] = ((both[:64] + both[64:]) * scale + off[...]).astype(BF16)
        return carry

    lax.fori_loop(0, 4, late, 0)

    for n, combo in enumerate(combos):
        me, far, near = scatter(n, *combo)

        @pl.when(jnp.logical_not(me))
        def _():
            far.wait_send()

    z_copy(0).wait_send()
    z_copy(1).wait_send()

    @pl.when(src == 1)
    def _():
        z_copy(2).wait_send()

    for p in range(3):
        @pl.when(passing[p])
        def _():
            onward(p).wait_send()
    for p in range(4):
        for kind in range(3):
            x_copy(p, kind).wait_send()
    for g in range(8):
        ring_a(0, g).wait_send()
        ring_a(1, g).wait_send()
        ring_b(g).wait_send()
    for kind in range(4):
        for n in range(2):
            here(kind, n).wait_send()


def per_device(embedding, gain, shift, projector, final, offset):
    dma = pltpu.SemaphoreType.DMA
    operands = (jnp.swapaxes(embedding, 0, 1), gain.reshape(1, -1), shift.reshape(1, -1), projector.T, final, offset.reshape(1, -1))
    return pl.pallas_call(
        kernel,
        out_shape=jax.ShapeDtypeStruct((32, 64, 128), BF16),
        in_specs=[pl.BlockSpec(memory_space=pltpu.VMEM)] * 6,
        out_specs=pl.BlockSpec(memory_space=pltpu.VMEM),
        scratch_shapes=[
            pltpu.VMEM((2, 1024, 256), BF16),
            pltpu.VMEM((4, 32, 64, 128), BF16),
            pltpu.VMEM((128, 256), BF16),
            pltpu.VMEM((2, 4, 32, 128), BF16),
            pltpu.VMEM((2, 512, 128), BF16),
            pltpu.VMEM((8, 128, 128), F32),
            pltpu.VMEM((1024, 128), F32),
            pltpu.VMEM((4, 256, 128), BF16),
            pltpu.VMEM((4, 512, 1024), BF16),
            pltpu.VMEM((4, 128, 1024), F32),
            dma((3,)), dma((4,)), dma((3,)), dma((12,)), dma((12,)), dma((32,)), dma((32,)),
            dma((16,)), dma((16,)), dma((8,)), dma((8,)), dma((8,)), dma((8,)),
        ],
        compiler_params=pltpu.CompilerParams(
            collective_id=0, has_side_effects=True, vmem_limit_bytes=48 << 20
        ),
    )(*operands)


def solution(mesh):
    in_specs = (P("seq", ("ri", "rj"), None), P(), P(), P(), P(), P())
    return jax.shard_map(
        per_device, mesh=mesh, in_specs=in_specs, out_specs=P(("ri", "seq"), "rj", None), check_vma=False
    )
```

time: 54.9 us -> 51.6 us (0.940)
  Pallas kernels: 52.1 us -> 48.8 us
    pallas_call x1, Pallas kernels: 52.1 us -> 48.8 us  [per_device(): pl.pallas_call(kernel, out_shape=jax.ShapeDtypeStruct((32, 64, 128), BF16...]
where the time goes in v2:
time: 51.6 us; the launch traced here: 51.5 us
  Pallas kernels  48.8 us (95%)
  local copies, waits for them, and re-layouts  2.6 us (5%)
    pallas_call x1, Pallas kernels, per_device(): pl.pallas_call(kernel, out_shape=jax.ShapeDtypeStruct((32, 64, 128), BF16...  48.8 us
    unnamed x12, local copies, waits for them, and re-layouts  2.6 us

profile of v2, /device:TPU:1, one launch (start us, length us, event | category | flops | bytes accessed | tf_op | source)
XLA Modules:
  0.0 51.5 jit_solution(18386652842759815686)
XLA Ops:
  0.0 0.0 copy-start
  0.0 0.0 copy-start.1
  0.0 0.0 copy-start.3
  0.0 1.2 %copy.9 = bf16[256,4,256]{2,0,1:T(8,128)(2,1)S(1)} copy(bf16[256,4,256]{2,1,0:T(4,128)(2,1)} %param.6) | data formatting | bytes 1048576 | tf_op args[0]
  1.2 0.0 copy-start.2
  1.2 0.0 copy-start.4
  1.2 0.0 copy-done
  1.2 0.0 copy-done.1
  1.2 0.0 copy-done.3
  1.2 0.6 %copy-done.2 = f32[256]{0:T(256)S(1)} copy-done((f32[256]{0:T(256)S(1)}, f32[256]{0:T(256)}, u32[]{:S(2)}) %copy-start.2) | copy-done | bytes 1048
  1.9 0.0 copy-done.4
  1.9 48.8 %shard_map.64 = bf16[32,64,128]{2,1,0:T(8,128)(2,1)S(1)} custom-call(bf16[4,256,256]{2,1,0:T(8,128)(2,1)S(1)} %bitcast.7, f32[1,256]{1,0:T(1,128)S(1)} %bitcast.9, f32[1,256]{1,0:T(1,128)S(1)} %bitcast.10, bf16[64,256]{1,0:T(8,128)(2,1)S(1)} %bitcast.8, bf16[1024,128]{1,0:T(8,128)(2,1)S(1)} %copy-done, f32[1,128]{1,0:T(1,128)S(1)} %bitcast.11), custom_call_target="tpu_custom_call" | custom-call | tf_op jit(solution)/shard_map/pallas_call | solution.py:348
  50.7 0.8 %copy.11 = bf16[32,64,128]{2,1,0:T(8,128)(2,1)} copy(bf16[32,64,128]{2,1,0:T(8,128)(2,1)S(1)} %shard_map.64) | data formatting | bytes 1048576
Async XLA Ops:
  0.0 1.2 %copy-start = (bf16[1024,128]{1,0:T(8,128)(2,1)S(1)}, bf16[1024,128]{1,0:T(8,128)(2,1)}, u32[]{:S(2)}) copy-start(bf16[1024,128]{1,0:T(8,128)(2,1)} %wfin.1) | copy-start | bytes 786436
  0.0 1.2 %copy-start.1 = (bf16[256,64]{0,1:T(8,128)(2,1)S(1)}, bf16[256,64]{0,1:T(8,128)(2,1)}, u32[]{:S(2)}) copy-start(bf16[256,64]{0,1:T(8,128)(2,1)} %param.9) | copy-start | bytes 98308
  0.0 1.2 %copy-start.3 = (f32[256]{0:T(256)S(1)}, f32[256]{0:T(256)}, u32[]{:S(2)}) copy-start(f32[256]{0:T(256)} %param.8) | copy-start | bytes 3076
  1.2 0.7 %copy-start.2 = (f32[256]{0:T(256)S(1)}, f32[256]{0:T(256)}, u32[]{:S(2)}) copy-start(f32[256]{0:T(256)} %param.7) | copy-start | bytes 3076
  1.2 0.7 %copy-start.4 = (f32[128]{0:T(128)S(1)}, f32[128]{0:T(128)}, u32[]{:S(2)}) copy-start(f32[128]{0:T(128)} %param.11) | copy-start | bytes 1540

commit v3 on v2

--- a/solution.py
+++ b/solution.py
@@ -34,7 +34,7 @@
     for dc in range(4):
         rows = jnp.concatenate([p[dc * 8:(dc + 1) * 8] for p in pieces], axis=0).astype(BF16)
         for sl in range(2):
-            rsend[sl, dc] = rows[:, sl * 128:(sl + 1) * 128]
+            rsend[dc, sl] = rows[:, sl * 128:(sl + 1) * 128]
 
 
 def arrange_final(wfin, wide, w2t):
@@ -66,14 +66,15 @@
 
 
 def kernel(x_ref, gain, shift, w64, wfin, off, out,
-           lt, rt, lsend, rsend, stage, stage_f, wide, w2t, outer, partial,
-           z_send, z_recv, f_send, x_send, x_recv, s_send, s_recv, a_send, a_recv, b_send, b_recv, p_send, p_recv):
+           lt, rt, lsend, rsend, mid, stage, stage_f, wide, w2t, outer, partial,
+           z_send, z_recv, f_send, x_send, x_recv, m_send, m_recv, s_send, s_recv, a_send, a_recv, b_send, b_recv, p_send, p_recv):
     q, ri, rj = lax.axis_index("seq"), lax.axis_index("ri"), lax.axis_index("rj")
     y, c, zl, xx = ri // 2, ri % 2, rj // 4, rj % 4
     half = zl // 2
     way = 1 - 2 * c
     self_z = half == q
-    self_s = rj == ri
+    self_s = c == rj % 2
+    self_s_count = jnp.where(self_s, 1, 0)
 
     def at_x(n):
         return (q, ri, zl * 4 + (xx + n + 4) % 4)
@@ -99,10 +100,12 @@
 
             @pl.when(jnp.logical_not(me))
             def _():
-                greet((a, rj, s))
+                greet((a, 2 * y + rj % 2, s))
 
         return carry
 
+    for n in (4, 3, -3, 2, -2, 1, -1):
+        greet(at_y(n))
     lax.fori_loop(0, 16, greet_source, 0)
 
     def greet_place(w):
@@ -122,34 +125,23 @@
     greet_place(table(-1, -1, 3, 2))
     for n in (1, -1):
         greet(at_x(n))
-        greet(at_y(n))
     greet(peer)
 
     project(x_ref, gain, shift, w64, lsend, rsend)
 
     z_targets = jnp.where(src == 1, 3, 2) + jnp.where(place == 2, 2, 1)
-    pl.semaphore_wait(barrier, 32 - self_s.astype(jnp.int32) + z_targets + 5)
-
-    def scatter(n, dc, sl, qd, yh):
-        dev = (qd, 2 * (dc + 4 * yh) + sl, ri)
-        me = jnp.logical_and(jnp.logical_and(qd == q, rj == ri), 2 * (dc + 4 * yh) + sl == ri)
-        dst = stage.at[q, pl.ds(pl.multiple_of(rj * 32, 32), 32), :]
-        sem = s_recv.at[q * 16 + rj]
-        return me, remote(rsend.at[sl, dc], dst, s_send.at[n], sem, dev), pltpu.make_async_copy(
-            rsend.at[sl, dc], dst, sem
-        )
-
-    combos = [(dc, sl, qd, yh) for dc in range(4) for sl in range(2) for qd in range(2) for yh in range(2)]
-    for n, combo in enumerate(combos):
-        me, far, near = scatter(n, *combo)
-
-        @pl.when(me)
-        def _():
-            near.start()
-
-        @pl.when(jnp.logical_not(me))
-        def _():
-            far.start()
+    pl.semaphore_wait(barrier, 32 - self_s_count + 7 + z_targets + 3)
+
+    mid_slot = mid.at[y]
+
+    def along_y(n):
+        to = (y + n + 8) % 8
+        return remote(rsend.at[to % 4], mid_slot, m_send.at[n % 8], m_recv.at[y], at_y(n))
+
+    for n in (4, 3, -3, 2, -2, 1, -1):
+        along_y(n).start()
+    own_mid = pltpu.make_async_copy(rsend.at[y % 4], mid_slot, m_recv.at[y])
+    own_mid.start()
 
     def left_slot(h, e, x):
         a = e // 2 + h - 2 * (e // 2) * h
@@ -174,6 +166,32 @@
     @pl.when(self_z)
     def _():
         pltpu.make_async_copy(lsend, z_slot, z_recv.at[own]).start()
+
+    def in_plane(n, sl, qd):
+        ys = (y + n + 8) % 8
+        dev = (qd, 2 * y + sl, 2 * ys + c)
+        me = jnp.logical_and(jnp.logical_and(qd == q, sl == c), 2 * ys + c == rj)
+        dst = stage.at[q, pl.ds(pl.multiple_of(rj * 32, 32), 32), :]
+        sem = s_recv.at[q * 16 + rj]
+        at = (n % 8) * 4 + sl * 2 + qd
+        return me, remote(mid.at[ys, sl], dst, s_send.at[at], sem, dev), pltpu.make_async_copy(mid.at[ys, sl], dst, sem)
+
+    hops = (0, 1, -1, 2, -2, 3, -3, 4)
+
+    def spread(n):
+        ys = (y + n + 8) % 8
+        pltpu.make_async_copy(mid.at[ys], mid.at[ys], m_recv.at[ys]).wait()
+        for sl in range(2):
+            for qd in range(2):
+                me, far, near = in_plane(n, sl, qd)
+
+                @pl.when(me)
+                def _():
+                    near.start()
+
+                @pl.when(jnp.logical_not(me))
+                def _():
+                    far.start()
 
     arrange_final(wfin, wide, w2t)
 
@@ -266,18 +284,30 @@
             here(1, g // 4).start()
             here(2, g // 4).start()
 
+    spread(0)
+    spread(1)
+    spread(-1)
     z_land(0)
+    spread(2)
+    spread(-2)
     z_land(1)
+    spread(3)
+    spread(-3)
+    spread(4)
+    z_land(2)
+    x_step(0)
     for g in range(4):
         assemble(g)
-    z_land(2)
+    x_step(1)
+    z_land(3)
     for g in range(4, 8):
         assemble(g)
-    z_land(3)
-    for g in range(8):
+    x_step(2)
+    for g in range(4):
         pass_on(g)
-        if g % 2 == 1:
-            x_step(g // 2)
+    x_step(3)
+    for g in range(4, 8):
+        pass_on(g)
     for p in range(4):
         x_land(p, 1)
         x_land(p, 2)
@@ -286,13 +316,11 @@
 
     dcs = [(y + n) % 4 for n in (0, 1, 3, 2)]
 
-    def early(ib, carry):
-        for pos in range(3):
+    for pos in range(3):
+        for ib in range(4):
             outer_product(ib, pos, dcs[pos], lt, rt, outer)
+    for ib in range(4):
         partial[ib] = last_product(ib, 0, dcs[:2], w2t, outer)
-        return carry
-
-    lax.fori_loop(0, 4, early, 0)
 
     for g in range(8):
         land(a_recv.at[8 + g], part(-way * 2, g))
@@ -302,22 +330,24 @@
 
     scale = 1.0 / (2 * x_ref.shape[1])
 
-    def late(ib, carry):
+    for ib in range(4):
         outer_product(ib, 3, dcs[3], lt, rt, outer)
+    for ib in range(4):
         total = partial[ib] + last_product(ib, 1, dcs[2:], w2t, outer)
         for i in range(8):
             both = total[:, i * 128:(i + 1) * 128].T
             out[ib * 8 + i] = ((both[:64] + both[64:]) * scale + off[...]).astype(BF16)
-        return carry
-
-    lax.fori_loop(0, 4, late, 0)
-
-    for n, combo in enumerate(combos):
-        me, far, near = scatter(n, *combo)
-
-        @pl.when(jnp.logical_not(me))
-        def _():
-            far.wait_send()
+
+    for n in hops:
+        if n:
+            along_y(n).wait_send()
+        for sl in range(2):
+            for qd in range(2):
+                me, far, near = in_plane(n, sl, qd)
+
+                @pl.when(jnp.logical_not(me))
+                def _():
+                    far.wait_send()
 
     z_copy(0).wait_send()
     z_copy(1).wait_send()
@@ -354,14 +384,15 @@
             pltpu.VMEM((2, 1024, 256), BF16),
             pltpu.VMEM((4, 32, 64, 128), BF16),
             pltpu.VMEM((128, 256), BF16),
-            pltpu.VMEM((2, 4, 32, 128), BF16),
+            pltpu.VMEM((4, 2, 32, 128), BF16),
+            pltpu.VMEM((8, 2, 32, 128), BF16),
             pltpu.VMEM((2, 512, 128), BF16),
             pltpu.VMEM((8, 128, 128), F32),
             pltpu.VMEM((1024, 128), F32),
             pltpu.VMEM((4, 256, 128), BF16),
             pltpu.VMEM((4, 512, 1024), BF16),
             pltpu.VMEM((4, 128, 1024), F32),
-            dma((3,)), dma((4,)), dma((3,)), dma((12,)), dma((12,)), dma((32,)), dma((32,)),
+            dma((3,)), dma((4,)), dma((3,)), dma((12,)), dma((12,)), dma((8,)), dma((8,)), dma((32,)), dma((32,)),
             dma((16,)), dma((16,)), dma((8,)), dma((8,)), dma((8,)), dma((8,)),
         ],
         compiler_params=pltpu.CompilerParams(

time: 51.6 us -> 47.1 us (0.913)
  Pallas kernels: 48.8 us -> 43.9 us
    pallas_call x1, Pallas kernels: 48.8 us -> 43.9 us  [per_device(): pl.pallas_call(kernel, out_shape=jax.ShapeDtypeStruct((32, 64, 128), BF16...]
where the time goes in v3:
time: 47.1 us; the launch traced here: 46.6 us
  Pallas kernels  43.9 us (93%)
  local copies, waits for them, and re-layouts  2.6 us (6%)
    pallas_call x1, Pallas kernels, per_device(): pl.pallas_call(kernel, out_shape=jax.ShapeDtypeStruct((32, 64, 128), BF16...  43.9 us
    unnamed x12, local copies, waits for them, and re-layouts  2.6 us

profile of v3, /device:TPU:1, one launch (start us, length us, event | category | flops | bytes accessed | tf_op | source)
XLA Modules:
  0.0 46.6 jit_solution(2751256925228138204)
XLA Ops:
  0.0 0.0 copy-start
  0.0 0.0 copy-start.1
  0.0 0.0 copy-start.3
  0.0 1.2 %copy.9 = bf16[256,4,256]{2,0,1:T(8,128)(2,1)S(1)} copy(bf16[256,4,256]{2,1,0:T(4,128)(2,1)} %param.6) | data formatting | bytes 1048576 | tf_op args[0]
  1.2 0.0 copy-start.2
  1.2 0.0 copy-start.4
  1.2 0.0 copy-done
  1.2 0.0 copy-done.1
  1.2 0.0 copy-done.3
  1.2 0.6 %copy-done.2 = f32[256]{0:T(256)S(1)} copy-done((f32[256]{0:T(256)S(1)}, f32[256]{0:T(256)}, u32[]{:S(2)}) %copy-start.2) | copy-done | bytes 1048
  1.9 0.0 copy-done.4
  1.9 43.9 %shard_map.64 = bf16[32,64,128]{2,1,0:T(8,128)(2,1)S(1)} custom-call(bf16[4,256,256]{2,1,0:T(8,128)(2,1)S(1)} %bitcast.7, f32[1,256]{1,0:T(1,128)S(1)} %bitcast.9, f32[1,256]{1,0:T(1,128)S(1)} %bitcast.10, bf16[64,256]{1,0:T(8,128)(2,1)S(1)} %bitcast.8, bf16[1024,128]{1,0:T(8,128)(2,1)S(1)} %copy-done, f32[1,128]{1,0:T(1,128)S(1)} %bitcast.11), custom_call_target="tpu_custom_call" | custom-call | tf_op jit(solution)/shard_map/pallas_call | solution.py:378
  45.8 0.8 %copy.11 = bf16[32,64,128]{2,1,0:T(8,128)(2,1)} copy(bf16[32,64,128]{2,1,0:T(8,128)(2,1)S(1)} %shard_map.64) | data formatting | bytes 1048576
Async XLA Ops:
  0.0 1.2 %copy-start = (bf16[1024,128]{1,0:T(8,128)(2,1)S(1)}, bf16[1024,128]{1,0:T(8,128)(2,1)}, u32[]{:S(2)}) copy-start(bf16[1024,128]{1,0:T(8,128)(2,1)} %wfin.1) | copy-start | bytes 786436
  0.0 1.2 %copy-start.1 = (bf16[256,64]{0,1:T(8,128)(2,1)S(1)}, bf16[256,64]{0,1:T(8,128)(2,1)}, u32[]{:S(2)}) copy-start(bf16[256,64]{0,1:T(8,128)(2,1)} %param.9) | copy-start | bytes 98308
  0.0 1.2 %copy-start.3 = (f32[256]{0:T(256)S(1)}, f32[256]{0:T(256)}, u32[]{:S(2)}) copy-start(f32[256]{0:T(256)} %param.8) | copy-start | bytes 3076
  1.2 0.7 %copy-start.2 = (f32[256]{0:T(256)S(1)}, f32[256]{0:T(256)}, u32[]{:S(2)}) copy-start(f32[256]{0:T(256)} %param.7) | copy-start | bytes 3076
  1.2 0.7 %copy-start.4 = (f32[128]{0:T(128)S(1)}, f32[128]{0:T(128)}, u32[]{:S(2)}) copy-start(f32[128]{0:T(128)} %param.11) | copy-start | bytes 1540

commit v4 on v3

--- a/solution.py
+++ b/solution.py
@@ -94,7 +94,7 @@
     def greet(dev):
         pl.semaphore_signal(barrier, inc=1, device_id=dev, device_id_type=MESH)
 
-    def greet_source(s, carry):
+    for s in range(16):
         for a in range(2):
             me = jnp.logical_and(self_s, jnp.logical_and(a == q, s == rj))
 
@@ -102,11 +102,8 @@
             def _():
                 greet((a, 2 * y + rj % 2, s))
 
-        return carry
-
     for n in (4, 3, -3, 2, -2, 1, -1):
         greet(at_y(n))
-    lax.fori_loop(0, 16, greet_source, 0)
 
     def greet_place(w):
         @pl.when(w >= 0)
@@ -308,6 +305,28 @@
     x_step(3)
     for g in range(4, 8):
         pass_on(g)
+    for n in hops:
+        if n:
+            along_y(n).wait_send()
+        for sl in range(2):
+            for qd in range(2):
+                me, far, near = in_plane(n, sl, qd)
+
+                @pl.when(jnp.logical_not(me))
+                def _():
+                    far.wait_send()
+
+    z_copy(0).wait_send()
+    z_copy(1).wait_send()
+
+    @pl.when(src == 1)
+    def _():
+        z_copy(2).wait_send()
+
+    for p in range(3):
+        @pl.when(passing[p])
+        def _():
+            onward(p).wait_send()
     for p in range(4):
         x_land(p, 1)
         x_land(p, 2)
@@ -321,6 +340,16 @@
             outer_product(ib, pos, dcs[pos], lt, rt, outer)
     for ib in range(4):
         partial[ib] = last_product(ib, 0, dcs[:2], w2t, outer)
+
+    for p in range(4):
+        for kind in range(3):
+            x_copy(p, kind).wait_send()
+    for g in range(8):
+        ring_a(0, g).wait_send()
+        ring_b(g).wait_send()
+    for kind in range(3):
+        for n in range(2):
+            here(kind, n).wait_send()
 
     for g in range(8):
         land(a_recv.at[8 + g], part(-way * 2, g))
@@ -338,38 +367,10 @@
             both = total[:, i * 128:(i + 1) * 128].T
             out[ib * 8 + i] = ((both[:64] + both[64:]) * scale + off[...]).astype(BF16)
 
-    for n in hops:
-        if n:
-            along_y(n).wait_send()
-        for sl in range(2):
-            for qd in range(2):
-                me, far, near = in_plane(n, sl, qd)
-
-                @pl.when(jnp.logical_not(me))
-                def _():
-                    far.wait_send()
-
-    z_copy(0).wait_send()
-    z_copy(1).wait_send()
-
-    @pl.when(src == 1)
-    def _():
-        z_copy(2).wait_send()
-
-    for p in range(3):
-        @pl.when(passing[p])
-        def _():
-            onward(p).wait_send()
-    for p in range(4):
-        for kind in range(3):
-            x_copy(p, kind).wait_send()
     for g in range(8):
-        ring_a(0, g).wait_send()
         ring_a(1, g).wait_send()
-        ring_b(g).wait_send()
-    for kind in range(4):
-        for n in range(2):
-            here(kind, n).wait_send()
+    for n in range(2):
+        here(3, n).wait_send()
 
 
 def per_device(embedding, gain, shift, projector, final, offset):

time: 47.1 us -> 47 us (level)
  no operation moved by 1% of the time
where the time goes in v4:
time: 47 us; the launch traced here: 46.4 us
  Pallas kernels  43.7 us (93%)
  local copies, waits for them, and re-layouts  2.6 us (6%)
    pallas_call x1, Pallas kernels, per_device(): pl.pallas_call(kernel, out_shape=jax.ShapeDtypeStruct((32, 64, 128), BF16...  43.7 us
    unnamed x12, local copies, waits for them, and re-layouts  2.6 us

profile of v4, /device:TPU:1, one launch (start us, length us, event | category | flops | bytes accessed | tf_op | source)
XLA Modules:
  0.0 46.4 jit_solution(18173785291696045927)
XLA Ops:
  0.0 0.0 copy-start
  0.0 0.0 copy-start.1
  0.0 0.0 copy-start.3
  0.0 1.2 %copy.9 = bf16[256,4,256]{2,0,1:T(8,128)(2,1)S(1)} copy(bf16[256,4,256]{2,1,0:T(4,128)(2,1)} %param.6) | data formatting | bytes 1048576 | tf_op args[0]
  1.2 0.0 copy-start.2
  1.2 0.0 copy-start.4
  1.2 0.0 copy-done
  1.2 0.0 copy-done.1
  1.2 0.0 copy-done.3
  1.2 0.6 %copy-done.2 = f32[256]{0:T(256)S(1)} copy-done((f32[256]{0:T(256)S(1)}, f32[256]{0:T(256)}, u32[]{:S(2)}) %copy-start.2) | copy-done | bytes 1048
  1.9 0.0 copy-done.4
  1.9 43.7 %shard_map.64 = bf16[32,64,128]{2,1,0:T(8,128)(2,1)S(1)} custom-call(bf16[4,256,256]{2,1,0:T(8,128)(2,1)S(1)} %bitcast.7, f32[1,256]{1,0:T(1,128)S(1)} %bitcast.9, f32[1,256]{1,0:T(1,128)S(1)} %bitcast.10, bf16[64,256]{1,0:T(8,128)(2,1)S(1)} %bitcast.8, bf16[1024,128]{1,0:T(8,128)(2,1)S(1)} %copy-done, f32[1,128]{1,0:T(1,128)S(1)} %bitcast.11), custom_call_target="tpu_custom_call" | custom-call | tf_op jit(solution)/shard_map/pallas_call | solution.py:379
  45.6 0.8 %copy.11 = bf16[32,64,128]{2,1,0:T(8,128)(2,1)} copy(bf16[32,64,128]{2,1,0:T(8,128)(2,1)S(1)} %shard_map.64) | data formatting | bytes 1048576
Async XLA Ops:
  0.0 1.2 %copy-start = (bf16[1024,128]{1,0:T(8,128)(2,1)S(1)}, bf16[1024,128]{1,0:T(8,128)(2,1)}, u32[]{:S(2)}) copy-start(bf16[1024,128]{1,0:T(8,128)(2,1)} %wfin.1) | copy-start | bytes 786436
  0.0 1.2 %copy-start.1 = (bf16[256,64]{0,1:T(8,128)(2,1)S(1)}, bf16[256,64]{0,1:T(8,128)(2,1)}, u32[]{:S(2)}) copy-start(bf16[256,64]{0,1:T(8,128)(2,1)} %param.9) | copy-start | bytes 98308
  0.0 1.2 %copy-start.3 = (f32[256]{0:T(256)S(1)}, f32[256]{0:T(256)}, u32[]{:S(2)}) copy-start(f32[256]{0:T(256)} %param.8) | copy-start | bytes 3076
  1.2 0.7 %copy-start.2 = (f32[256]{0:T(256)S(1)}, f32[256]{0:T(256)}, u32[]{:S(2)}) copy-start(f32[256]{0:T(256)} %param.7) | copy-start | bytes 3076
  1.2 0.7 %copy-start.4 = (f32[128]{0:T(128)S(1)}, f32[128]{0:T(128)}, u32[]{:S(2)}) copy-start(f32[128]{0:T(128)} %param.11) | copy-start | bytes 1540

commit v5 on v4

--- a/solution.py
+++ b/solution.py
@@ -120,14 +120,14 @@
     greet_place(table(5, 4, 1, 4))
     greet_place(table(1, 0, 5, 2))
     greet_place(table(-1, -1, 3, 2))
-    for n in (1, -1):
+    for n in (1, -1, 2):
         greet(at_x(n))
     greet(peer)
 
     project(x_ref, gain, shift, w64, lsend, rsend)
 
     z_targets = jnp.where(src == 1, 3, 2) + jnp.where(place == 2, 2, 1)
-    pl.semaphore_wait(barrier, 32 - self_s_count + 7 + z_targets + 3)
+    pl.semaphore_wait(barrier, 32 - self_s_count + 7 + z_targets + 4)
 
     mid_slot = mid.at[y]
 
@@ -195,6 +195,8 @@
     order = [table(0, 1, 1, 2), table(1, 0, 0, 1), table(3, 2, 3, 0), table(2, 3, 2, 3)]
     passing = [place == 3, place == 2, place <= 2]
 
+    straight = (3,)
+
     def onward(p):
         e = order[p]
         s = left_slot(q, e, xx)
@@ -202,8 +204,13 @@
 
     def x_copy(p, kind):
         e = order[p]
-        s = left_slot(q, e, xx if kind < 2 else (xx - way + 4) % 4)
-        return remote(s, s, x_send.at[e * 3 + kind], x_recv.at[e * 3 + kind], at_x(-way if kind == 1 else way))
+        if kind == 2 and p in straight:
+            s, n = left_slot(q, e, xx), 2
+        elif kind == 2:
+            s, n = left_slot(q, e, (xx - way + 4) % 4), way
+        else:
+            s, n = left_slot(q, e, xx), (way, -way)[kind]
+        return remote(s, s, x_send.at[e * 3 + kind], x_recv.at[e * 3 + kind], at_x(n))
 
     def x_land(p, kind):
         e = order[p]
@@ -220,10 +227,13 @@
                 onward(p).start()
         x_copy(p, 0).start()
         x_copy(p, 1).start()
+        if p in straight:
+            x_copy(p, 2).start()
 
     def x_step(p):
         x_land(p, 0)
-        x_copy(p, 2).start()
+        if p not in straight:
+            x_copy(p, 2).start()
 
     near_zl = (zl, zl + 1 - 2 * (zl % 2), (zl + 2) % 4, 3 - zl)
     parts = [(q, near_zl[n]) for n in (0, 1, 2, 3)] + [(1 - q, near_zl[n]) for n in (3, 2, 1, 0)]
@@ -293,18 +303,16 @@
     spread(4)
     z_land(2)
     x_step(0)
-    for g in range(4):
+    for g in range(0, 4):
         assemble(g)
     x_step(1)
     z_land(3)
     for g in range(4, 8):
         assemble(g)
     x_step(2)
-    for g in range(4):
+    for g in range(0, 8):
         pass_on(g)
     x_step(3)
-    for g in range(4, 8):
-        pass_on(g)
     for n in hops:
         if n:
             along_y(n).wait_send()

time: 47 us -> 47 us (level)
  no operation moved by 1% of the time
where the time goes in v5:
time: 47 us; the launch traced here: 46.4 us
  Pallas kernels  43.7 us (93%)
  local copies, waits for them, and re-layouts  2.6 us (6%)
    pallas_call x1, Pallas kernels, per_device(): pl.pallas_call(kernel, out_shape=jax.ShapeDtypeStruct((32, 64, 128), BF16...  43.7 us
    unnamed x12, local copies, waits for them, and re-layouts  2.6 us

profile of v5, /device:TPU:1, one launch (start us, length us, event | category | flops | bytes accessed | tf_op | source)
XLA Modules:
  0.0 46.4 jit_solution(11195179398260697599)
XLA Ops:
  0.0 0.0 copy-start
  0.0 0.0 copy-start.1
  0.0 0.0 copy-start.3
  0.0 1.2 %copy.9 = bf16[256,4,256]{2,0,1:T(8,128)(2,1)S(1)} copy(bf16[256,4,256]{2,1,0:T(4,128)(2,1)} %param.6) | data formatting | bytes 1048576 | tf_op args[0]
  1.2 0.0 copy-start.2
  1.2 0.0 copy-start.4
  1.2 0.0 copy-done
  1.2 0.0 copy-done.1
  1.2 0.0 copy-done.3
  1.2 0.6 %copy-done.2 = f32[256]{0:T(256)S(1)} copy-done((f32[256]{0:T(256)S(1)}, f32[256]{0:T(256)}, u32[]{:S(2)}) %copy-start.2) | copy-done | bytes 1048
  1.9 0.0 copy-done.4
  1.9 43.7 %shard_map.64 = bf16[32,64,128]{2,1,0:T(8,128)(2,1)S(1)} custom-call(bf16[4,256,256]{2,1,0:T(8,128)(2,1)S(1)} %bitcast.7, f32[1,256]{1,0:T(1,128)S(1)} %bitcast.9, f32[1,256]{1,0:T(1,128)S(1)} %bitcast.10, bf16[64,256]{1,0:T(8,128)(2,1)S(1)} %bitcast.8, bf16[1024,128]{1,0:T(8,128)(2,1)S(1)} %copy-done, f32[1,128]{1,0:T(1,128)S(1)} %bitcast.11), custom_call_target="tpu_custom_call" | custom-call | tf_op jit(solution)/shard_map/pallas_call | solution.py:387
  45.6 0.8 %copy.11 = bf16[32,64,128]{2,1,0:T(8,128)(2,1)} copy(bf16[32,64,128]{2,1,0:T(8,128)(2,1)S(1)} %shard_map.64) | data formatting | bytes 1048576
Async XLA Ops:
  0.0 1.2 %copy-start = (bf16[1024,128]{1,0:T(8,128)(2,1)S(1)}, bf16[1024,128]{1,0:T(8,128)(2,1)}, u32[]{:S(2)}) copy-start(bf16[1024,128]{1,0:T(8,128)(2,1)} %wfin.1) | copy-start | bytes 786436
  0.0 1.2 %copy-start.1 = (bf16[256,64]{0,1:T(8,128)(2,1)S(1)}, bf16[256,64]{0,1:T(8,128)(2,1)}, u32[]{:S(2)}) copy-start(bf16[256,64]{0,1:T(8,128)(2,1)} %param.9) | copy-start | bytes 98308
  0.0 1.2 %copy-start.3 = (f32[256]{0:T(256)S(1)}, f32[256]{0:T(256)}, u32[]{:S(2)}) copy-start(f32[256]{0:T(256)} %param.8) | copy-start | bytes 3076
  1.2 0.7 %copy-start.2 = (f32[256]{0:T(256)S(1)}, f32[256]{0:T(256)}, u32[]{:S(2)}) copy-start(f32[256]{0:T(256)} %param.7) | copy-start | bytes 3076
  1.2 0.7 %copy-start.4 = (f32[128]{0:T(128)S(1)}, f32[128]{0:T(128)}, u32[]{:S(2)}) copy-start(f32[128]{0:T(128)} %param.11) | copy-start | bytes 1540
